TPU v7x, 32 devices: a whole 2x2x4 slice. The times are simulated.
32 devices in a mesh: beads: 8 (over y, x, core), waves: 4 (over z).
Axes of the slice: x: 2, y: 2, z: 4, core: 2. Of those that a mesh axis runs over, the one named last changes fastest.
Arguments:
- positions: float32 [3, 4096], P(None, 'beads'), may hold values from 0 to 256
- features: bfloat16 [4096, 256], P(('beads', 'waves')), may hold values from -6 to 6
- cotangent: bfloat16 [4096, 256], P(('beads', 'waves')), may hold values from -6 to 6
- wavevectors: float32 [3, 4096], replicated, may hold values from -0.25 to 0.25
- filter_gain: bfloat16 [4096, 256], P(('beads', 'waves')), may hold values from -6 to 6
Outputs:
- grad_features: bfloat16 [4096, 256], P(('beads', 'waves'))
- grad_positions: float32 [3, 4096], P(None, ('beads', 'waves'))
- grad_filter: float32 [4096, 256], P(('beads', 'waves'))
All inputs are finite; a program needn't handle non-finite values.
Results may differ from a plain program's by a relative error of at most 0.012.
Values may be sent and summed in bfloat16 or wider, within the bound.
A program may use at most 64 MiB of HBM per device.

v0:
```python
import math

import jax
import jax.numpy as jnp
from jax import lax
from jax.sharding import PartitionSpec as P


def phases(pos, kvec):
    return (
        pos[0][:, None] * kvec[0][None, :]
        + pos[1][:, None] * kvec[1][None, :]
        + pos[2][:, None] * kvec[2][None, :]
    )


def contract_rows(left, right):
    return lax.dot_general(
        left, right, (((1,), (1,)), ((), ())), preferred_element_type=jnp.float32
    )


def contract_cols(left, right):
    return lax.dot_general(
        left, right, (((0,), (0,)), ((), ())), preferred_element_type=jnp.float32
    )


def filtered_spectra(term, gains, width):
    spec_r = term[:, :width]
    spec_i = term[:, width : 2 * width]
    cot_r = term[:, 2 * width : 3 * width]
    cot_i = term[:, 3 * width :]
    grad_filter = cot_r * spec_r + cot_i * spec_i
    stacked = jnp.concatenate(
        [gains * spec_r, gains * spec_i, gains * cot_r, gains * cot_i], 1
    ).astype(jnp.bfloat16)
    return (stacked, grad_filter)


def body(positions, features, cotangent, wavevectors, filter_gain):
    n_beads = lax.axis_size("beads")
    n_waves = lax.axis_size("waves")
    feats, cots = (
        lax.all_gather(features, "waves", axis=0, tiled=True),
        lax.all_gather(cotangent, "waves", axis=0, tiled=True),
    )
    beads_dev = feats.shape[0]
    width = feats.shape[1]
    waves_all = wavevectors.shape[1]
    per_owner = waves_all // (n_beads * n_waves)
    waves_dev = per_owner * n_beads
    spec_scale = 1.0 / math.sqrt(beads_dev * n_beads)
    wave_scale = 1.0 / math.sqrt(waves_all)
    grid = wavevectors.reshape(3, n_beads, n_waves, per_owner)
    local_waves = lax.dynamic_slice_in_dim(grid, lax.axis_index("waves"), 1, 2).reshape(
        3, waves_dev
    )
    joined = jnp.concatenate([feats, cots], 1)
    block = min(512, waves_dev)
    turns = waves_dev // block

    def fold_step(carry, piece, start):
        grad_feat, grad_pos = carry
        count = piece.shape[0]
        kvec = lax.dynamic_slice_in_dim(local_waves, start, count, 1)
        theta = phases(positions, kvec)
        cosine = jnp.cos(theta).astype(jnp.bfloat16)
        sine = jnp.sin(theta).astype(jnp.bfloat16)
        filt_r = piece[:, :width]
        filt_i = piece[:, width : 2 * width]
        dspec_r = piece[:, 2 * width : 3 * width]
        dspec_i = piece[:, 3 * width :]
        feat_term = (
            jnp.dot(cosine, dspec_r, preferred_element_type=jnp.float32)
            + jnp.dot(sine, dspec_i, preferred_element_type=jnp.float32)
        ) * spec_scale
        first = (
            contract_rows(cots, filt_r) * wave_scale + contract_rows(feats, dspec_r) * spec_scale
        )
        second = (
            contract_rows(cots, filt_i) * wave_scale + contract_rows(feats, dspec_i) * spec_scale
        )
        dtheta = -sine.astype(jnp.float32) * first + cosine.astype(jnp.float32) * second
        pos_term = lax.dot_general(
            kvec,
            dtheta,
            (((1,), (1,)), ((), ())),
            precision=lax.Precision.HIGHEST,
            preferred_element_type=jnp.float32,
        )
        return (grad_feat + feat_term, grad_pos + pos_term)

    kvec = local_waves
    theta = phases(positions, kvec)
    cosine = jnp.cos(theta).astype(jnp.bfloat16)
    sine = jnp.sin(theta).astype(jnp.bfloat16)
    part_cos = contract_cols(cosine, joined)
    part_sin = contract_cols(sine, joined)
    term = lax.psum_scatter(
        jnp.concatenate(
            [
                part_cos[:, :width] * spec_scale,
                part_sin[:, :width] * spec_scale,
                part_cos[:, width:] * wave_scale,
                part_sin[:, width:] * wave_scale,
            ],
            1,
        ),
        "beads",
        scatter_dimension=0,
        tiled=True,
    )
    owned, grad_filter = filtered_spectra(term, filter_gain.astype(jnp.float32), width)
    stacked = lax.all_gather(owned, "beads", axis=0, tiled=True)

    def sweep(step, carry):
        piece = lax.dynamic_slice_in_dim(stacked, step * block, block, 0)
        return fold_step(carry, piece, step * block)

    initial = (jnp.zeros((beads_dev, width), jnp.float32), jnp.zeros((3, beads_dev), jnp.float32))
    grads = lax.fori_loop(0, turns, sweep, initial)
    grad_feat, grad_pos = (
        lax.psum_scatter(
            grads[0].astype(jnp.bfloat16), "waves", scatter_dimension=0, tiled=True
        ).astype(jnp.float32),
        lax.psum_scatter(
            grads[1].astype(jnp.bfloat16), "waves", scatter_dimension=1, tiled=True
        ).astype(jnp.float32),
    )
    return (grad_feat.astype(jnp.bfloat16), grad_pos, grad_filter)


def solution(mesh):
    placed = (
        P(None, "beads"),
        P(("beads", "waves"), None),
        P(("beads", "waves"), None),
        P(),
        P(("beads", "waves"), None),
    )
    return jax.shard_map(
        body,
        mesh=mesh,
        in_specs=placed,
        out_specs=(
            P(("beads", "waves"), None),
            P(None, ("beads", "waves")),
            P(("beads", "waves"), None),
        ),
        check_vma=False,
    )
```

profile of v0, /device:TPU:0, one launch (start us, length us, event | category | flops | bytes accessed | tf_op | source)
XLA Modules:
  0.0 241.3 jit_solution(17202812354688805211)
XLA Ops:
  8.1 15.8 %all_gather.9 = bf16[512,256]{1,0:T(8,128)(2,1)S(1)} all-gather(bf16[128,256]{1,0:T(8,128)(2,1)} %param.8), channel_id=1, replica_groups=mesh['beads'=8,'waves'=4] {'waves'}, dimensions={0}, use_global_device_ids=true | all-gather | bytes 327680 | tf_op jit(solution)/shard_map/all_gather | solution.py:45
  24.0 14.8 %all_gather.10 = bf16[512,256]{1,0:T(8,128)(2,1)S(1)} all-gather(bf16[128,256]{1,0:T(8,128)(2,1)} %param.9), channel_id=1, replica_groups=mesh['beads'=8,'waves'=4] {'waves'}, dimensions={0}, use_global_device_ids=true | all-gather | bytes 327680 | tf_op jit(solution)/shard_map/all_gather | solution.py:46
  39.7 7.6 %fusion.21 = f32[1024,512]{0,1:T(8,128)S(1)} fusion(bf16[512,512]{1,0:T(8,128)(2,1)S(1)} %constant_dynamic-update-slice_fusion, f32[1024]{0:T(1024)S(1)} %get-tuple-element.230, f32[512]{0:T(512)S(1)} %bitcast.100, f32[1024]{0:T(1024)S(1)} %get-tuple-element.229, f32[512]{0:T(512)S(1)} %bitcast.98, f32[1024]{0:T(1024)S(1)} %get-tuple-element.228, ...), kind=kOutput, calls=%fused_computation.33 | convolution fusion | flops 540016640 | bytes 2639872 | tf_op jit(solution)/shard_map/dot_general | solution.py:24
  47.2 7.8 %fusion.22 = f32[1024,512]{0,1:T(8,128)S(1)} fusion(bf16[512,512]{1,0:T(8,128)(2,1)S(1)} %constant_dynamic-update-slice_fusion, f32[1024]{0:T(1024)S(1)} %get-tuple-element.230, f32[512]{0:T(512)S(1)} %bitcast.101, f32[1024]{0:T(1024)S(1)} %get-tuple-element.229, f32[512]{0:T(512)S(1)} %bitcast.99, f32[1024]{0:T(1024)S(1)} %get-tuple-element.228, ...), kind=kOutput, calls=%fused_computation.34 | convolution fusion | flops 540016640 | bytes 2639872 | tf_op jit(solution)/shard_map/dot_general | solution.py:24
  55.5 2.5 %pad_maximum_fusion = f32[1024,1024]{0,1:T(8,128)} fusion(f32[1024,256]{0,1:T(8,128)S(1)} %get-tuple-element.222, f32[1024,256]{0,1:T(8,128)S(1)} %get-tuple-element.234, f32[1024,256]{0,1:T(8,128)S(1)} %get-tuple-element.221, f32[1024,256]{0,1:T(8,128)S(1)} %get-tuple-element.235), kind=kLoop, calls=%fused_computation.29 | loop fusion | flops 3145728 | bytes 8388608 | tf_op jit(solution)/shard_map/concatenate | solution.py:101
  59.0 51.5 %reduce-scatter.6.cloned.1.call-done = f32[128,1024]{0,1:T(8,128)} async-done(((f32[1024,1024]{0,1:T(8,128)}), f32[128,1024]{0,1:T(8,128)}) %reduce-scatter.6.cloned.1.call-update) | async-done | bytes 524304 | tf_op jit(solution)/shard_map/reduce_scatter | solution.py:100
  112.5 28.3 %all-gather.2.cloned.1.call-done = bf16[1024,1024]{0,1:T(8,128)(2,1)} async-done(((bf16[128,1024]{0,1:T(8,128)(2,1)}), bf16[1024,1024]{0,1:T(8,128)(2,1)}) %all-gather.2.cloned.1.call-update) | async-done | bytes 2097168 | tf_op jit(solution)/shard_map/all_gather | solution.py:115
  140.8 52.6 %while.16 = (s32[]{:T(128)}, f32[512,256]{1,0:T(8,128)}, f32[3,512]{1,0:T(4,128)}, f32[3,512]{1,0:T(4,128)}, f32[3,1024]{1,0:T(4,128)S(1)}, /*index=5*/bf16[1024...) while((s32[]{:T(128)}, f32[512,256]{1,0:T(8,128)}, ...), condition=%wide.region_2.0_spmd.clone, body=%wide.region_1.0_spmd.clone.sunk | while | flops 824183808 | bytes 15397590 | solution.py:122
  141.7 1.2 fusion.80
  143.0 4.7 %fusion.81 = f32[512,512]{1,0:T(8,128)S(1)} fusion(f32[512,512]{0,1:T(8,128)S(1)} %fusion.80, bf16[512,256]{1,0:T(8,128)(2,1)S(1)} %get-tuple-element.338, f32[512]{0:T(512)S(1)} %bitcast.73, f32[512]{0:T(512)S(1)} %bitcast.85, f32[512]{0:T(512)S(1)} %bitcast.77, f32[512]{0:T(512)S(1)} %bitcast.81, f32[512]{0:T(512)S(1)} %bitcast.69, ...), kind=kOutput, calls=%fused_computation.8.clone.1 | convolution fusion | flops 136839168 | bytes 2633736 | tf_op jit(solution)/shard_map/while/body/eval_jaxpr/dot_general | solution.py:18
  147.7 1.2 fusion.82
  148.9 5.2 %fusion.83 = f32[512,512]{1,0:T(8,128)S(1)} fusion(f32[512,512]{1,0:T(8,128)S(1)} %fusion.81, f32[512,512]{0,1:T(8,128)S(1)} %fusion.82, bf16[512,256]{1,0:T(8,128)(2,1)} %copy-done, f32[512]{0:T(512)} %bitcast.74, f32[512]{0:T(512)} %bitcast.86, f32[512]{0:T(512)} %bitcast.78, f32[512]{0:T(512)} %bitcast.82, f32[512]{0:T(512)} %bitcast.70, ...), kind=kOutput, calls=%fused_computation.7.clone.1 | convolution fusion | flops 137363456 | bytes 3682312 | tf_op jit(solution)/shard_map/while/body/eval_jaxpr/dot_general | solution.py:18
  154.2 1.6 convolution_add_fusion.5
  155.8 4.8 %fusion.78 = f32[512,256]{1,0:T(8,128)S(1)} fusion(f32[512]{0:T(512)} %bitcast.75, f32[512]{0:T(512)} %bitcast.87, f32[512]{0:T(512)} %bitcast.79, f32[512]{0:T(512)} %bitcast.83, f32[512]{0:T(512)} %bitcast.71, f32[512]{0:T(512)} %bitcast.91, bf16[1024,1024]{0,1:T(8,128)(2,1)} %get-tuple-element.336, s32[]{:T(128)S(6)} %select_n.14, s32[]{:T(128)S(6)} %add.223), kind=kOutput, calls=%fused_computation.16.clone.1 | convolution fusion | flops 135790592 | bytes 798728 | tf_op jit(solution)/shard_map/while/body/eval_jaxpr/dot_general | solution.py:75
  160.6 6.1 %fusion.79 = f32[512,256]{1,0:T(8,128)} fusion(f32[512,256]{1,0:T(8,128)S(1)} %fusion.78, f32[512,256]{1,0:T(8,128)} %get-tuple-element.315, f32[512]{0:T(512)S(1)} %bitcast.76, f32[512]{0:T(512)S(1)} %bitcast.88, f32[512]{0:T(512)S(1)} %bitcast.80, f32[512]{0:T(512)S(1)} %bitcast.84, f32[512]{0:T(512)S(1)} %bitcast.72, f32[512]{0:T(512)S(1)} %bitcast.92, ...), kind=kOutput, calls=%fused_computation.11.clone.1 | convolution fusion | flops 136314880 | bytes 1847305 | tf_op jit(solution)/shard_map/while/body/eval_jaxpr/dot_general | solution.py:76
  167.6 1.2 fusion.80
  169.0 4.7 %fusion.81 = f32[512,512]{1,0:T(8,128)S(1)} fusion(f32[512,512]{0,1:T(8,128)S(1)} %fusion.80, bf16[512,256]{1,0:T(8,128)(2,1)S(1)} %get-tuple-element.338, f32[512]{0:T(512)S(1)} %bitcast.73, f32[512]{0:T(512)S(1)} %bitcast.85, f32[512]{0:T(512)S(1)} %bitcast.77, f32[512]{0:T(512)S(1)} %bitcast.81, f32[512]{0:T(512)S(1)} %bitcast.69, ...), kind=kOutput, calls=%fused_computation.8.clone.1 | convolution fusion | flops 136839168 | bytes 2633736 | tf_op jit(solution)/shard_map/while/body/eval_jaxpr/dot_general | solution.py:18
  174.9 5.2 %fusion.83 = f32[512,512]{1,0:T(8,128)S(1)} fusion(f32[512,512]{1,0:T(8,128)S(1)} %fusion.81, f32[512,512]{0,1:T(8,128)S(1)} %fusion.82, bf16[512,256]{1,0:T(8,128)(2,1)} %copy-done, f32[512]{0:T(512)} %bitcast.74, f32[512]{0:T(512)} %bitcast.86, f32[512]{0:T(512)} %bitcast.78, f32[512]{0:T(512)} %bitcast.82, f32[512]{0:T(512)} %bitcast.70, ...), kind=kOutput, calls=%fused_computation.7.clone.1 | convolution fusion | flops 137363456 | bytes 3682312 | tf_op jit(solution)/shard_map/while/body/eval_jaxpr/dot_general | solution.py:18
  180.1 2.3 convolution_add_fusion.5
  182.4 4.8 %fusion.78 = f32[512,256]{1,0:T(8,128)S(1)} fusion(f32[512]{0:T(512)} %bitcast.75, f32[512]{0:T(512)} %bitcast.87, f32[512]{0:T(512)} %bitcast.79, f32[512]{0:T(512)} %bitcast.83, f32[512]{0:T(512)} %bitcast.71, f32[512]{0:T(512)} %bitcast.91, bf16[1024,1024]{0,1:T(8,128)(2,1)} %get-tuple-element.336, s32[]{:T(128)S(6)} %select_n.14, s32[]{:T(128)S(6)} %add.223), kind=kOutput, calls=%fused_computation.16.clone.1 | convolution fusion | flops 135790592 | bytes 798728 | tf_op jit(solution)/shard_map/while/body/eval_jaxpr/dot_general | solution.py:75
  187.2 6.2 %fusion.79 = f32[512,256]{1,0:T(8,128)} fusion(f32[512,256]{1,0:T(8,128)S(1)} %fusion.78, f32[512,256]{1,0:T(8,128)} %get-tuple-element.315, f32[512]{0:T(512)S(1)} %bitcast.76, f32[512]{0:T(512)S(1)} %bitcast.88, f32[512]{0:T(512)S(1)} %bitcast.80, f32[512]{0:T(512)S(1)} %bitcast.84, f32[512]{0:T(512)S(1)} %bitcast.72, f32[512]{0:T(512)S(1)} %bitcast.92, ...), kind=kOutput, calls=%fused_computation.11.clone.1 | convolution fusion | flops 136314880 | bytes 1847305 | tf_op jit(solution)/shard_map/while/body/eval_jaxpr/dot_general | solution.py:76
  195.0 1.8 convert_element_type.52
  197.6 16.7 %reduce-scatter.10.cloned.1.call-done = bf16[128,3]{1,0:T(8,128)(2,1)} async-done(((bf16[512,3]{1,0:T(8,128)(2,1)}), bf16[128,3]{1,0:T(8,128)(2,1)}) %reduce-scatter.10.cloned.1.call-update) | async-done | bytes 784
  215.7 19.0 %reduce-scatter.8.cloned.1.call-done = bf16[128,256]{1,0:T(8,128)(2,1)} async-done(((bf16[512,256]{1,0:T(8,128)(2,1)}), bf16[128,256]{1,0:T(8,128)(2,1)}) %reduce-scatter.8.cloned.1.call-update) | async-done | bytes 65552 | tf_op jit(solution)/shard_map/reduce_scatter | solution.py:124
  (87 shorter events, 12.1 us)
Async XLA Ops:
  7.2 103.3 %reduce-scatter.6.cloned.1.call-start = ((), (), s32[]{:S(2)}) async-start(), calls=%async_computation.3 | async-start | bytes 4718592 | tf_op jit(solution)/shard_map/reduce_scatter | solution.py:100
  58.1 82.7 %all-gather.2.cloned.1.call-start = ((), (), s32[]{:S(2)}) async-start(), calls=%async_computation.4 | async-start | bytes 2359296 | tf_op jit(solution)/shard_map/all_gather | solution.py:115
  112.4 101.9 %reduce-scatter.10.cloned.1.call-start = ((), (), s32[]{:S(2)}) async-start(), calls=%async_computation.6 | async-start | bytes 163840
  140.8 2.2 copy-start
  141.7 1.3 copy-start.8
  141.7 1.3 copy-start.10
  154.1 6.4 %copy-start.3 = (f32[1,512]{1,0:T(1,128)S(1)}, f32[1,512]{1,0:T(1,128)}, u32[]{:S(2)}) copy-start(f32[1,512]{1,0:T(1,128)} %copy-done.2) | copy-start | bytes 6148 | tf_op jit(solution)/shard_map/while
  154.1 6.4 %copy-start.5 = (f32[1,512]{1,0:T(1,128)S(1)}, f32[1,512]{1,0:T(1,128)}, u32[]{:S(2)}) copy-start(f32[1,512]{1,0:T(1,128)} %copy-done.4) | copy-start | bytes 6148 | tf_op jit(solution)/shard_map/while
  154.1 6.4 %copy-start.7 = (f32[1,512]{1,0:T(1,128)S(1)}, f32[1,512]{1,0:T(1,128)}, u32[]{:S(2)}) copy-start(f32[1,512]{1,0:T(1,128)} %copy-done.6) | copy-start | bytes 6148 | tf_op jit(solution)/shard_map/while
  154.2 6.4 %copy-start.9 = (f32[1,512]{1,0:T(1,128)S(1)}, f32[1,512]{1,0:T(1,128)}, u32[]{:S(2)}) copy-start(f32[1,512]{1,0:T(1,128)} %copy-done.8) | copy-start | bytes 6148 | tf_op jit(solution)/shard_map/while
  154.2 6.4 %copy-start.11 = (f32[1,512]{1,0:T(1,128)S(1)}, f32[1,512]{1,0:T(1,128)}, u32[]{:S(2)}) copy-start(f32[1,512]{1,0:T(1,128)} %copy-done.10) | copy-start | bytes 6148 | tf_op jit(solution)/shard_map/while
  154.2 6.4 %copy-start.13 = (f32[1,512]{1,0:T(1,128)S(1)}, f32[1,512]{1,0:T(1,128)}, u32[]{:S(2)}) copy-start(f32[1,512]{1,0:T(1,128)} %copy-done.12) | copy-start | bytes 6148 | tf_op jit(solution)/shard_map/while
  155.8 10.9 %copy-start.1 = (bf16[512,256]{1,0:T(8,128)(2,1)S(1)}, bf16[512,256]{1,0:T(8,128)(2,1)}, u32[]{:S(2)}) copy-start(bf16[512,256]{1,0:T(8,128)(2,1)} %copy-done) | copy-start | bytes 786436 | tf_op jit(solution)/shard_map/while
  166.7 2.2 copy-start
  167.6 1.3 copy-start.8
  167.6 1.3 copy-start.10
  180.1 7.1 %copy-start.3 = (f32[1,512]{1,0:T(1,128)S(1)}, f32[1,512]{1,0:T(1,128)}, u32[]{:S(2)}) copy-start(f32[1,512]{1,0:T(1,128)} %copy-done.2) | copy-start | bytes 6148 | tf_op jit(solution)/shard_map/while
  180.1 7.1 %copy-start.5 = (f32[1,512]{1,0:T(1,128)S(1)}, f32[1,512]{1,0:T(1,128)}, u32[]{:S(2)}) copy-start(f32[1,512]{1,0:T(1,128)} %copy-done.4) | copy-start | bytes 6148 | tf_op jit(solution)/shard_map/while
  180.1 7.1 %copy-start.7 = (f32[1,512]{1,0:T(1,128)S(1)}, f32[1,512]{1,0:T(1,128)}, u32[]{:S(2)}) copy-start(f32[1,512]{1,0:T(1,128)} %copy-done.6) | copy-start | bytes 6148 | tf_op jit(solution)/shard_map/while
  180.1 7.1 %copy-start.9 = (f32[1,512]{1,0:T(1,128)S(1)}, f32[1,512]{1,0:T(1,128)}, u32[]{:S(2)}) copy-start(f32[1,512]{1,0:T(1,128)} %copy-done.8) | copy-start | bytes 6148 | tf_op jit(solution)/shard_map/while
  180.1 7.1 %copy-start.11 = (f32[1,512]{1,0:T(1,128)S(1)}, f32[1,512]{1,0:T(1,128)}, u32[]{:S(2)}) copy-start(f32[1,512]{1,0:T(1,128)} %copy-done.10) | copy-start | bytes 6148 | tf_op jit(solution)/shard_map/while
  180.1 7.1 %copy-start.13 = (f32[1,512]{1,0:T(1,128)S(1)}, f32[1,512]{1,0:T(1,128)}, u32[]{:S(2)}) copy-start(f32[1,512]{1,0:T(1,128)} %copy-done.12) | copy-start | bytes 6148 | tf_op jit(solution)/shard_map/while
  182.4 11.0 %copy-start.1 = (bf16[512,256]{1,0:T(8,128)(2,1)S(1)}, bf16[512,256]{1,0:T(8,128)(2,1)}, u32[]{:S(2)}) copy-start(bf16[512,256]{1,0:T(8,128)(2,1)} %copy-done) | copy-start | bytes 786436 | tf_op jit(solution)/shard_map/while
  194.9 39.8 %reduce-scatter.8.cloned.1.call-start = ((), (), s32[]{:S(2)}) async-start(), calls=%async_computation.5 | async-start | bytes 327680 | tf_op jit(solution)/shard_map/reduce_scatter | solution.py:124
  (9 other events, 11.3 us)
Sparse Core Ops, SparseCore 0:
  58.2 52.2 reduce-scatter.5
  112.5 28.1 all-gather.1
  195.1 19.1 reduce-scatter.9
  217.0 17.7 reduce-scatter.7
where the time goes:
time: 242 us; the launch traced here: 241 us
  waiting for transfers between devices  116 us (48%)
  matrix products  65.7 us (27%)
  blocking collectives  30.7 us (13%)
  between operations  13.8 us (6%)
  other arithmetic  7.95 us (3%)
  local copies, waits for them, and re-layouts  6.96 us (3%)
    reduce_scatter x1, waiting for transfers between devices, body(): lax.psum_scatter(jnp.concatenate([part_cos[:, :width] * spec_scale, part_...  51.5 us
    all_gather x1, waiting for transfers between devices, body(): stacked = lax.all_gather(owned, 'beads', axis=0, tiled=True)  28.3 us
    dot_general x8, matrix products, contract_rows(): lax.dot_general(left, right, (((1,), (1,)), ((), ())), preferred_element_...  24.7 us
    reduce_scatter x1, waiting for transfers between devices, body(): lax.psum_scatter(grads[0].astype(jnp.bfloat16), 'waves', scatter_dimensio...  19 us
    unnamed x5, waiting for transfers between devices  16.8 us
    all_gather x1, blocking collectives, body(): lax.all_gather(features, 'waves', axis=0, tiled=True)  15.8 us
    dot_general x2, matrix products, contract_cols(): lax.dot_general(left, right, (((0,), (0,)), ((), ())), preferred_element_...  15.4 us
    all_gather x1, blocking collectives, body(): lax.all_gather(cotangent, 'waves', axis=0, tiled=True)  14.8 us
  transfers between devices with their start and end apart: 4, of which 4 were waited for; matrix products, arithmetic and copies ran while one was open for 2% of the time, Pallas kernels for 0%

commit v1 on v0

--- a/solution.py
+++ b/solution.py
@@ -1,9 +1,306 @@
+import functools
 import math
 
 import jax
 import jax.numpy as jnp
 from jax import lax
+from jax.experimental import pallas as pl
+from jax.experimental.pallas import tpu as pltpu
 from jax.sharding import PartitionSpec as P
+
+MESH = pl.DeviceIdType.MESH
+PLANE = 4
+LANES = 128
+
+
+def flip(i, q):
+    out = i
+    if q % 2:
+        out = out + 1 - 2 * (i % 2)
+    if q // 2:
+        out = out + 2 - 4 * ((i // 2) % 2)
+    return out
+
+
+def sincos(theta):
+    n = jnp.round(theta * (2.0 / math.pi))
+    k = n.astype(jnp.int32)
+    r = (theta - n * 1.5703125) - n * 4.83826794896619e-4
+    r2 = r * r
+    s = r + r * r2 * (-1.6666654611e-1 + r2 * (8.3321608736e-3 - r2 * 1.9515295891e-4))
+    c = (1.0 - 0.5 * r2) + r2 * r2 * (
+        4.166664568298827e-2 + r2 * (-1.388731625493765e-3 + r2 * 2.443315711809948e-5)
+    )
+    swap = (k & 1) == 1
+    sv = jnp.where(swap, c, s)
+    cv = jnp.where(swap, s, c)
+    sv = jnp.where((k & 2) == 2, -sv, sv)
+    cv = jnp.where(((k + 1) & 2) == 2, -cv, cv)
+    return cv, sv
+
+
+def kernel(
+    nz, spec_scale, wave_scale,
+    pos_ref, feat_ref, cot_ref, kvec_ref, gain_ref,
+    gfeat_ref, gpos_ref, gfilt_ref,
+    pos_all, joined, kcol, cs, acc, mid_tx, mid_rx, ebuf, dt, pf, sb, rx, rz,
+    send_sem, recv_sem,
+):
+    own = feat_ref.shape[0]
+    width = feat_ref.shape[1]
+    per = gain_ref.shape[0]
+    block = nz * own
+    kk = 2 * per
+    b = lax.axis_index("beads")
+    z = lax.axis_index("waves")
+    core = b % 2
+    plane = b // 2
+    partner = (b + 1 - 2 * core, z)
+    near = [None] + [(flip(plane, r) * 2 + core, z) for r in range(1, PLANE)]
+    far = [None] + [(b, flip(z, q)) for q in range(1, nz)]
+    zq = [flip(z, q) for q in range(nz)]
+    peers = [partner] + near[1:] + far[1:]
+
+    barrier = pltpu.get_barrier_semaphore()
+    for peer in peers:
+        pl.semaphore_signal(barrier, inc=1, device_id=peer, device_id_type=MESH)
+
+    ids = {}
+    pending = []
+
+    def copy(name, src, dst, to):
+        i = ids.setdefault(name, len(ids))
+        return pltpu.make_async_remote_copy(
+            src_ref=src, dst_ref=dst, send_sem=send_sem.at[i], recv_sem=recv_sem.at[i],
+            device_id=to, device_id_type=MESH,
+        )
+
+    def send(name, src, dst, to):
+        c = copy(name, src, dst, to)
+        c.start()
+        pending.append(c)
+        return c
+
+    def rows(q):
+        return pl.ds(pl.multiple_of(zq[q] * own, own), own)
+
+    pos_all[0] = pos_ref[...]
+    joined[0, rows(0), :width] = feat_ref[...]
+    joined[0, rows(0), width:] = cot_ref[...]
+    pl.semaphore_wait(barrier, len(peers))
+
+    got = {}
+    for r in range(1, PLANE):
+        got["p", r] = send(("p", r), pos_all.at[0], pos_all.at[r], near[r])
+
+    def hop(r, q, src, to):
+        got[r, q] = send((r, q), joined.at[src, rows(q)], joined.at[r, rows(q)], to)
+
+    hop(1, 0, 0, near[1])
+    hop(2, 0, 0, near[2])
+    for q in range(1, nz):
+        got[0, q] = send((0, q), joined.at[0, rows(0)], joined.at[0, rows(0)], far[q])
+
+    eye = lax.broadcasted_iota(jnp.int32, (per, per), 0) == lax.broadcasted_iota(
+        jnp.int32, (per, per), 1
+    )
+    for g in range(2):
+        owner = (b + g * (1 - 2 * core)) * nz + z
+        piece = kvec_ref[:, pl.ds(pl.multiple_of(owner * per, per), per)]
+        for d in range(3):
+            line = jnp.where(eye, jnp.broadcast_to(piece[d : d + 1], (per, per)), 0.0)
+            kcol[d, g * per : (g + 1) * per, :] = jnp.broadcast_to(
+                jnp.sum(line, axis=1, keepdims=True), (per, LANES)
+            )
+
+    step = 16
+    per_group = per // step
+    wide = block // LANES
+
+    def waves(r):
+        p = pos_all[r]
+
+        def one(i, _):
+            at = pl.ds(pl.multiple_of(i * step, step), step)
+            k0, k1, k2 = (jnp.concatenate([kcol[d, at, :]] * wide, 1) for d in range(3))
+            theta = p[0:1] * k0 + p[1:2] * k1 + p[2:3] * k2
+            cv, sv = sincos(theta)
+            base = (i // per_group) * kk + (i % per_group) * step
+            cs[r, pl.ds(pl.multiple_of(base, step), step), :] = cv.astype(jnp.bfloat16)
+            cs[r, pl.ds(pl.multiple_of(base + per, step), step), :] = sv.astype(jnp.bfloat16)
+            return 0
+
+        lax.fori_loop(0, 2 * per_group, one, 0)
+
+    def spread(r, first):
+        term = jnp.dot(cs[r], joined[r], preferred_element_type=jnp.float32)
+        if first:
+            acc[...] = term
+        else:
+            acc[...] += term
+
+    def arrive(r, q):
+        got[r, q].wait_recv()
+
+    half = nz // 2
+    waves(0)
+    arrive(2, 0)
+    hop(3, 0, 2, near[1])
+    for q in range(1, nz):
+        arrive(0, q)
+        hop(1, q, 0, near[1])
+        hop(2, q, 0, near[2])
+        if q == 1:
+            spread_ready = True
+        arrive(1, q - 1)
+        if q >= 2:
+            arrive(2, q - 1)
+        if q < half:
+            pass
+        if q - 1 >= half:
+            hop(3, q - 1, 1, near[2])
+        elif q - 1 > 0:
+            hop(3, q - 1, 2, near[1])
+        if q < PLANE:
+            got["p", q].wait_recv()
+            waves(q)
+    spread(0, True)
+    arrive(1, nz - 1)
+    arrive(2, nz - 1)
+    hop(3, nz - 1, 1, near[2])
+    spread(1, False)
+    spread(2, False)
+    for q in range(nz):
+        arrive(3, q)
+    spread(3, False)
+
+    mid_tx[...] = acc[kk:, :].astype(jnp.bfloat16)
+    first = send("m1", mid_tx, mid_rx, partner)
+    first.wait_recv()
+    total = acc[:kk, :] + mid_rx[...].astype(jnp.float32)
+    gain = gain_ref[...].astype(jnp.float32)
+    sr, gr = total[:per, :width] * spec_scale, total[:per, width:] * wave_scale
+    si, gi = total[per:, :width] * spec_scale, total[per:, width:] * wave_scale
+    gfilt_ref[...] = gr * sr + gi * si
+    ebuf[:per, :width] = (gain * gr * spec_scale).astype(jnp.bfloat16)
+    ebuf[:per, width:] = (gain * sr * wave_scale).astype(jnp.bfloat16)
+    ebuf[per:kk, :width] = (gain * gi * spec_scale).astype(jnp.bfloat16)
+    ebuf[per:kk, width:] = (gain * si * wave_scale).astype(jnp.bfloat16)
+    second = send("m2", ebuf.at[:kk], ebuf.at[kk:], partner)
+    second.wait_recv()
+    dt[...] = jnp.transpose(ebuf[:, :width].astype(jnp.float32)).astype(jnp.bfloat16)
+
+    tall = pf.shape[2]
+    cols = 2 * own
+    halves = block // cols
+
+    def fold(r):
+        def one(h, _):
+            at = pl.ds(pl.multiple_of(h * cols, cols), cols)
+            trig = cs[r, :, at]
+            grad = jnp.dot(dt[...], trig, preferred_element_type=jnp.float32)
+            ab = lax.dot_general(
+                ebuf[...], joined[r, at, :], (((1,), (1,)), ((), ())),
+                preferred_element_type=jnp.float32,
+            )
+            sums = [jnp.zeros((1, cols), jnp.float32)] * 3
+            for g in range(2):
+                lo = g * kk
+                dth = (
+                    trig[lo : lo + per].astype(jnp.float32) * ab[lo + per : lo + kk]
+                    - trig[lo + per : lo + kk].astype(jnp.float32) * ab[lo : lo + per]
+                )
+                for d in range(3):
+                    k = jnp.concatenate([kcol[d, g * per : (g + 1) * per, :]] * (cols // LANES), 1)
+                    sums[d] = sums[d] + jnp.sum(dth * k, axis=0, keepdims=True)
+            rest = jnp.zeros((tall - width - 3, cols), jnp.float32)
+            tail = jnp.concatenate(sums + [rest], 0)
+            for j in range(2):
+                lane = slice(j * own, (j + 1) * own)
+                pf[r, h * 2 + j, :width, :] = grad[:, lane]
+                pf[r, h * 2 + j, width:, :] = tail[:, lane]
+            return 0
+
+        lax.fori_loop(0, halves, one, 0)
+
+    def give(r, q, to, dst, *extra):
+        value = pf[r, zq[q]]
+        for e in extra:
+            value = value + e[...].astype(jnp.float32)
+        sb[r, q] = value.astype(jnp.bfloat16)
+        got["g", r, q] = send(("g", r, q), sb.at[r, q], dst, to)
+
+    fold(3)
+    for q in reversed(range(nz)):
+        give(3, q, near[1] if q < half else near[2], rx.at[2, q])
+    fold(1)
+    fold(2)
+    for q in reversed(range(nz)):
+        if q >= half:
+            give(2, q, near[2], rx.at[1, q])
+            got["g", 3, q].wait_recv()
+            give(1, q, near[1], rx.at[0, q], rx.at[2, q])
+        else:
+            give(1, q, near[1], rx.at[0, q])
+            got["g", 3, q].wait_recv()
+            give(2, q, near[2], rx.at[1, q], rx.at[2, q])
+    fold(0)
+    for q in reversed(range(1, nz)):
+        got["g", 1, q].wait_recv()
+        got["g", 2, q].wait_recv()
+        give(0, q, far[q], rz.at[q], rx.at[0, q], rx.at[1, q])
+    got["g", 1, 0].wait_recv()
+    got["g", 2, 0].wait_recv()
+    out = pf[0, zq[0]] + rx[0, 0].astype(jnp.float32) + rx[1, 0].astype(jnp.float32)
+    for q in reversed(range(1, nz)):
+        got["g", 0, q].wait_recv()
+        out = out + rz[q].astype(jnp.float32)
+    gfeat_ref[...] = jnp.transpose(out[:width]).astype(jnp.bfloat16)
+    gpos_ref[...] = out[width : width + 3]
+    for c in pending:
+        c.wait_send()
+
+
+def fused(nz, beads_all, positions, features, cotangent, wavevectors, filter_gain):
+    own, width = features.shape
+    per = filter_gain.shape[0]
+    block = nz * own
+    tall = width + 16
+    copies = 3 + PLANE * nz + 2 + PLANE * nz
+    spec_scale = 1.0 / math.sqrt(beads_all)
+    wave_scale = 1.0 / math.sqrt(wavevectors.shape[1])
+    bf, f32 = jnp.bfloat16, jnp.float32
+    vmem = pl.BlockSpec(memory_space=pltpu.VMEM)
+    return pl.pallas_call(
+        functools.partial(kernel, nz, spec_scale, wave_scale),
+        out_shape=(
+            jax.ShapeDtypeStruct((own, width), bf),
+            jax.ShapeDtypeStruct((3, own), f32),
+            jax.ShapeDtypeStruct((per, width), f32),
+        ),
+        in_specs=[vmem] * 5,
+        out_specs=(vmem,) * 3,
+        scratch_shapes=[
+            pltpu.VMEM((PLANE, 3, block), f32),
+            pltpu.VMEM((PLANE, block, 2 * width), bf),
+            pltpu.VMEM((3, 2 * per, LANES), f32),
+            pltpu.VMEM((PLANE, 4 * per, block), bf),
+            pltpu.VMEM((4 * per, 2 * width), f32),
+            pltpu.VMEM((2 * per, 2 * width), bf),
+            pltpu.VMEM((2 * per, 2 * width), bf),
+            pltpu.VMEM((4 * per, 2 * width), bf),
+            pltpu.VMEM((width, 4 * per), bf),
+            pltpu.VMEM((PLANE, nz, tall, own), f32),
+            pltpu.VMEM((PLANE, nz, tall, own), bf),
+            pltpu.VMEM((3, nz, tall, own), bf),
+            pltpu.VMEM((nz, tall, own), bf),
+            pltpu.SemaphoreType.DMA((copies,)),
+            pltpu.SemaphoreType.DMA((copies,)),
+        ],
+        compiler_params=pltpu.CompilerParams(
+            collective_id=0, has_side_effects=True, vmem_limit_bytes=40 << 20
+        ),
+    )(positions, features, cotangent, wavevectors, filter_gain)
 
 
 def phases(pos, kvec):
@@ -131,6 +428,10 @@
     return (grad_feat.astype(jnp.bfloat16), grad_pos, grad_filter)
 
 
+def suits(mesh):
+    return mesh.shape["beads"] == 2 * PLANE and mesh.shape["waves"] == PLANE
+
+
 def solution(mesh):
     placed = (
         P(None, "beads"),
@@ -139,14 +440,21 @@
         P(),
         P(("beads", "waves"), None),
     )
-    return jax.shard_map(
-        body,
-        mesh=mesh,
-        in_specs=placed,
-        out_specs=(
-            P(("beads", "waves"), None),
-            P(None, ("beads", "waves")),
-            P(("beads", "waves"), None),
-        ),
-        check_vma=False,
-    )
+
+    def run(positions, features, *rest):
+        part = body
+        if suits(mesh):
+            part = functools.partial(fused, mesh.shape["waves"], features.shape[0])
+        return jax.shard_map(
+            part,
+            mesh=mesh,
+            in_specs=placed,
+            out_specs=(
+                P(("beads", "waves"), None),
+                P(None, ("beads", "waves")),
+                P(("beads", "waves"), None),
+            ),
+            check_vma=False,
+        )(positions, features, *rest)
+
+    return run

time: 242 us -> 54.2 us (0.22)
  waiting for transfers between devices: 116 us -> 0 us
  matrix products: 65.7 us -> 0 us
  Pallas kernels: 0 us -> 47.3 us
  blocking collectives: 30.7 us -> 0 us
  between operations: 13.8 us -> 0.65 us
  other arithmetic: 7.95 us -> 0 us
    reduce_scatter x2 -> x0, waiting for transfers between devices: 70.5 us -> none  [the longest x1 51.5 us: body(): lax.psum_scatter(jnp.concatenate([part_cos[:, :width] * spec_scale, part_...]
    dot_general x16 -> x0, matrix products: 65.7 us -> none  [the longest x8 24.7 us: contract_rows(): lax.dot_general(left, right, (((1,), (1,)), ((), ())), preferred_element_...]
    pallas_call x0 -> x1, Pallas kernels: none -> 47.3 us  [fused(): pl.pallas_call(functools.partial(kernel, nz, spec_scale, wave_scale), out...]
    all_gather x2 -> x0, blocking collectives: 30.7 us -> none  [the longest x1 15.8 us: body(): lax.all_gather(features, 'waves', axis=0, tiled=True)]
    all_gather x1 -> x0, waiting for transfers between devices: 28.3 us -> none  [body(): stacked = lax.all_gather(owned, 'beads', axis=0, tiled=True)]
    unnamed x5 -> x0, waiting for transfers between devices: 16.8 us -> none
    concatenate x2 -> x0, other arithmetic: 3.27 us -> none  [the longest x1 2.54 us: body(): jnp.concatenate([part_cos[:, :width] * spec_scale, part_sin[:, :width] *...]
    convert_element_type x3 -> x0, other arithmetic: 3.09 us -> none  [the longest x1 1.78 us: body(): grads[0].astype(jnp.bfloat16)]
  transfers between devices with their start and end apart: 4 -> 0, of which waited for: 4 -> 0; matrix products, arithmetic and copies ran while one was open for 2% -> 0% of each run, Pallas kernels for 0% -> 0%
where the time goes in v1:
time: 54.2 us; the launch traced here: 53.9 us
  Pallas kernels  47.3 us (87%)
  local copies, waits for them, and re-layouts  5.91 us (11%)
  between operations  0.65 us (1%)
    pallas_call x1, Pallas kernels, fused(): pl.pallas_call(functools.partial(kernel, nz, spec_scale, wave_scale), out...  47.3 us
    unnamed x13, local copies, waits for them, and re-layouts  5.91 us

profile of v1, /device:TPU:0, one launch (start us, length us, event | category | flops | bytes accessed | tf_op | source)
XLA Modules:
  0.0 53.9 jit_solution(4316644262421690304)
XLA Ops:
  0.6 0.0 copy-start
  0.6 0.8 %copy-done = bf16[128,256]{1,0:T(8,128)(2,1)S(1)} copy-done((bf16[128,256]{1,0:T(8,128)(2,1)S(1)}, bf16[128,256]{1,0:T(8,128)(2,1)}, u32[]{:S(2)}) %copy-start) | copy-done | bytes 65560
  1.5 0.0 copy-start.1
  1.5 0.8 %copy-done.1 = bf16[128,256]{1,0:T(8,128)(2,1)S(1)} copy-done((bf16[128,256]{1,0:T(8,128)(2,1)S(1)}, bf16[128,256]{1,0:T(8,128)(2,1)}, u32[]{:S(2)}) %copy-start.1) | copy-done | bytes 65560
  2.3 0.0 copy-start.2
  2.3 0.8 %copy-done.2 = f32[3,4096]{1,0:T(4,128)S(1)} copy-done((f32[3,4096]{1,0:T(4,128)S(1)}, f32[3,4096]{1,0:T(4,128)}, u32[]{:S(2)}) %copy-start.2) | copy-done | bytes 49176
  3.2 0.0 copy-start.3
  3.2 0.8 %copy-done.3 = bf16[128,256]{1,0:T(8,128)(2,1)S(1)} copy-done((bf16[128,256]{1,0:T(8,128)(2,1)S(1)}, bf16[128,256]{1,0:T(8,128)(2,1)}, u32[]{:S(2)}) %copy-start.3) | copy-done | bytes 65560
  4.0 0.0 copy-start.4
  4.0 0.7 %copy-done.4 = f32[3,512]{1,0:T(4,128)S(1)} copy-done((f32[3,512]{1,0:T(4,128)S(1)}, f32[3,512]{1,0:T(4,128)}, u32[]{:S(2)}) %copy-start.4) | copy-done | bytes 6168
  4.7 47.3 %shard_map.76 = (bf16[128,256]{1,0:T(8,128)(2,1)S(1)}, f32[3,128]{1,0:T(4,128)S(1)}, f32[128,256]{1,0:T(8,128)S(1)}) custom-call(f32[3,512]{1,0:T(4,128)S(1)} %copy-done.4, bf16[128,256]{1,0:T(8,128)(2,1)S(1)} %copy-done, bf16[128,256]{1,0:T(8,128)(2,1)S(1)} %copy-done.1, f32[3,4096]{1,0:T(4,128)S(1)} %copy-done.2, bf16[128,256]{1,0:T(8,128)(2,1)S(1)} %copy-done.3), custom_call_target="tpu_custom_call" | custom-call | tf_op jit(solution)/shard_map/pallas_call | solution.py:274
  52.0 0.6 %copy.11 = bf16[128,256]{1,0:T(8,128)(2,1)} copy(bf16[128,256]{1,0:T(8,128)(2,1)S(1)} %get-tuple-element.6) | data formatting | bytes 131072
  52.7 0.6 %copy.12 = f32[3,128]{1,0:T(4,128)} copy(f32[3,128]{1,0:T(4,128)S(1)} %get-tuple-element.7) | data formatting | bytes 3072
  53.2 0.7 %copy.13 = f32[128,256]{1,0:T(8,128)} copy(f32[128,256]{1,0:T(8,128)S(1)} %get-tuple-element.8) | data formatting | bytes 262144
Async XLA Ops:
  0.6 0.8 %copy-start = (bf16[128,256]{1,0:T(8,128)(2,1)S(1)}, bf16[128,256]{1,0:T(8,128)(2,1)}, u32[]{:S(2)}) copy-start(bf16[128,256]{1,0:T(8,128)(2,1)} %feat_ref.1) | copy-start | bytes 196612
  1.5 0.8 %copy-start.1 = (bf16[128,256]{1,0:T(8,128)(2,1)S(1)}, bf16[128,256]{1,0:T(8,128)(2,1)}, u32[]{:S(2)}) copy-start(bf16[128,256]{1,0:T(8,128)(2,1)} %cot_ref.1) | copy-start | bytes 196612
  2.3 0.8 %copy-start.2 = (f32[3,4096]{1,0:T(4,128)S(1)}, f32[3,4096]{1,0:T(4,128)}, u32[]{:S(2)}) copy-start(f32[3,4096]{1,0:T(4,128)} %kvec_ref.1) | copy-start | bytes 147460
  3.2 0.8 %copy-start.3 = (bf16[128,256]{1,0:T(8,128)(2,1)S(1)}, bf16[128,256]{1,0:T(8,128)(2,1)}, u32[]{:S(2)}) copy-start(bf16[128,256]{1,0:T(8,128)(2,1)} %gain_ref.1) | copy-start | bytes 196612
  4.0 0.7 %copy-start.4 = (f32[3,512]{1,0:T(4,128)S(1)}, f32[3,512]{1,0:T(4,128)}, u32[]{:S(2)}) copy-start(f32[3,512]{1,0:T(4,128)} %pos_ref.1) | copy-start | bytes 18436

commit v2 on v1

--- a/solution.py
+++ b/solution.py
@@ -44,7 +44,7 @@
     pos_ref, feat_ref, cot_ref, kvec_ref, gain_ref,
     gfeat_ref, gpos_ref, gfilt_ref,
     pos_all, joined, kcol, cs, acc, mid_tx, mid_rx, ebuf, dt, pf, sb, rx, rz,
-    send_sem, recv_sem,
+    send_sem, recv_sem, local_sem, kvecs, gains,
 ):
     own = feat_ref.shape[0]
     width = feat_ref.shape[1]
@@ -84,10 +84,26 @@
     def rows(q):
         return pl.ds(pl.multiple_of(zq[q] * own, own), own)
 
-    pos_all[0] = pos_ref[...]
-    joined[0, rows(0), :width] = feat_ref[...]
-    joined[0, rows(0), width:] = cot_ref[...]
+    def part(q, j):
+        return pl.ds(pl.multiple_of(zq[q] * own + j * (own // 2), own // 2), own // 2)
+
+    loads = [
+        pltpu.make_async_copy(src, dst, local_sem.at[i])
+        for i, (src, dst) in enumerate(
+            [
+                (pos_ref, pos_all.at[0]),
+                (feat_ref, joined.at[0, rows(0), :width]),
+                (cot_ref, joined.at[0, rows(0), width:]),
+                (kvec_ref, kvecs),
+                (gain_ref, gains),
+            ]
+        )
+    ]
+    for c in loads:
+        c.start()
     pl.semaphore_wait(barrier, len(peers))
+    for c in loads[:3]:
+        c.wait()
 
     got = {}
     for r in range(1, PLANE):
@@ -98,15 +114,15 @@
 
     hop(1, 0, 0, near[1])
     hop(2, 0, 0, near[2])
-    for q in range(1, nz):
-        got[0, q] = send((0, q), joined.at[0, rows(0)], joined.at[0, rows(0)], far[q])
-
+    got[0, 1] = send((0, 1), joined.at[0, rows(0)], joined.at[0, rows(0)], far[1])
+
+    loads[3].wait()
     eye = lax.broadcasted_iota(jnp.int32, (per, per), 0) == lax.broadcasted_iota(
         jnp.int32, (per, per), 1
     )
     for g in range(2):
         owner = (b + g * (1 - 2 * core)) * nz + z
-        piece = kvec_ref[:, pl.ds(pl.multiple_of(owner * per, per), per)]
+        piece = kvecs[:, pl.ds(pl.multiple_of(owner * per, per), per)]
         for d in range(3):
             line = jnp.where(eye, jnp.broadcast_to(piece[d : d + 1], (per, per)), 0.0)
             kcol[d, g * per : (g + 1) * per, :] = jnp.broadcast_to(
@@ -143,34 +159,46 @@
         got[r, q].wait_recv()
 
     half = nz // 2
+
+    def post(q):
+        got[0, q] = send((0, q), joined.at[0, rows(0)], joined.at[0, rows(0)], far[q])
+
+    post(2)
+    post(3)
     waves(0)
     arrive(2, 0)
     hop(3, 0, 2, near[1])
-    for q in range(1, nz):
-        arrive(0, q)
-        hop(1, q, 0, near[1])
-        hop(2, q, 0, near[2])
-        if q == 1:
-            spread_ready = True
-        arrive(1, q - 1)
-        if q >= 2:
-            arrive(2, q - 1)
-        if q < half:
-            pass
-        if q - 1 >= half:
-            hop(3, q - 1, 1, near[2])
-        elif q - 1 > 0:
-            hop(3, q - 1, 2, near[1])
-        if q < PLANE:
-            got["p", q].wait_recv()
-            waves(q)
+    arrive(0, 1)
+    hop(1, 1, 0, near[1])
+    hop(2, 1, 0, near[2])
+    got["p", 1].wait_recv()
+    waves(1)
+    arrive(0, 2)
+    hop(1, 2, 0, near[1])
+    hop(2, 2, 0, near[2])
+    arrive(3, 0)
+    got[3, 1] = send((3, 1), joined.at[3, rows(0)], joined.at[3, rows(0)], far[1])
+    got["p", 2].wait_recv()
+    waves(2)
+    arrive(0, 3)
+    hop(1, 3, 0, near[1])
+    hop(2, 3, 0, near[2])
     spread(0, True)
-    arrive(1, nz - 1)
-    arrive(2, nz - 1)
-    hop(3, nz - 1, 1, near[2])
+    arrive(1, 2)
+    hop(3, 2, 1, near[2])
+    got["p", 3].wait_recv()
+    waves(3)
+    arrive(1, 3)
+    got[3, 3] = send((3, 3), joined.at[1, part(3, 0)], joined.at[3, part(3, 0)], near[2])
+    arrive(2, 3)
+    got[3, 4] = send((3, 4), joined.at[2, part(3, 1)], joined.at[3, part(3, 1)], near[1])
+    arrive(1, 0)
+    arrive(1, 1)
     spread(1, False)
+    arrive(2, 1)
+    arrive(2, 2)
     spread(2, False)
-    for q in range(nz):
+    for q in range(1, 5):
         arrive(3, q)
     spread(3, False)
 
@@ -178,7 +206,8 @@
     first = send("m1", mid_tx, mid_rx, partner)
     first.wait_recv()
     total = acc[:kk, :] + mid_rx[...].astype(jnp.float32)
-    gain = gain_ref[...].astype(jnp.float32)
+    loads[4].wait()
+    gain = gains[...].astype(jnp.float32)
     sr, gr = total[:per, :width] * spec_scale, total[:per, width:] * wave_scale
     si, gi = total[per:, :width] * spec_scale, total[per:, width:] * wave_scale
     gfilt_ref[...] = gr * sr + gi * si
@@ -266,7 +295,7 @@
     per = filter_gain.shape[0]
     block = nz * own
     tall = width + 16
-    copies = 3 + PLANE * nz + 2 + PLANE * nz
+    copies = 3 + PLANE * nz + 3 + PLANE * nz
     spec_scale = 1.0 / math.sqrt(beads_all)
     wave_scale = 1.0 / math.sqrt(wavevectors.shape[1])
     bf, f32 = jnp.bfloat16, jnp.float32
@@ -278,7 +307,7 @@
             jax.ShapeDtypeStruct((3, own), f32),
             jax.ShapeDtypeStruct((per, width), f32),
         ),
-        in_specs=[vmem] * 5,
+        in_specs=[pl.BlockSpec(memory_space=pltpu.HBM)] * 5,
         out_specs=(vmem,) * 3,
         scratch_shapes=[
             pltpu.VMEM((PLANE, 3, block), f32),
@@ -296,6 +325,9 @@
             pltpu.VMEM((nz, tall, own), bf),
             pltpu.SemaphoreType.DMA((copies,)),
             pltpu.SemaphoreType.DMA((copies,)),
+            pltpu.SemaphoreType.DMA((5,)),
+            pltpu.VMEM(wavevectors.shape, f32),
+            pltpu.VMEM((per, width), bf),
         ],
         compiler_params=pltpu.CompilerParams(
             collective_id=0, has_side_effects=True, vmem_limit_bytes=40 << 20

time: 54.2 us -> 52.3 us (0.965)
  Pallas kernels: 47.3 us -> 45.3 us
    pallas_call x1, Pallas kernels: 47.3 us -> 45.3 us  [fused(): pl.pallas_call(functools.partial(kernel, nz, spec_scale, wave_scale), out...]
where the time goes in v2:
time: 52.3 us; the launch traced here: 51.9 us
  Pallas kernels  45.3 us (87%)
  local copies, waits for them, and re-layouts  5.91 us (11%)
  between operations  0.65 us (1%)
    pallas_call x1, Pallas kernels, fused(): pl.pallas_call(functools.partial(kernel, nz, spec_scale, wave_scale), out...  45.3 us
    unnamed x13, local copies, waits for them, and re-layouts  5.91 us

profile of v2, /device:TPU:0, one launch (start us, length us, event | category | flops | bytes accessed | tf_op | source)
XLA Modules:
  0.0 51.9 jit_solution(8831483035485299280)
XLA Ops:
  0.6 0.0 copy-start
  0.6 0.8 %copy-done = bf16[128,256]{1,0:T(8,128)(2,1)S(1)} copy-done((bf16[128,256]{1,0:T(8,128)(2,1)S(1)}, bf16[128,256]{1,0:T(8,128)(2,1)}, u32[]{:S(2)}) %copy-start) | copy-done | bytes 65560
  1.5 0.0 copy-start.1
  1.5 0.8 %copy-done.1 = bf16[128,256]{1,0:T(8,128)(2,1)S(1)} copy-done((bf16[128,256]{1,0:T(8,128)(2,1)S(1)}, bf16[128,256]{1,0:T(8,128)(2,1)}, u32[]{:S(2)}) %copy-start.1) | copy-done | bytes 65560
  2.3 0.0 copy-start.2
  2.3 0.8 %copy-done.2 = f32[3,4096]{1,0:T(4,128)S(1)} copy-done((f32[3,4096]{1,0:T(4,128)S(1)}, f32[3,4096]{1,0:T(4,128)}, u32[]{:S(2)}) %copy-start.2) | copy-done | bytes 49176
  3.2 0.0 copy-start.3
  3.2 0.8 %copy-done.3 = bf16[128,256]{1,0:T(8,128)(2,1)S(1)} copy-done((bf16[128,256]{1,0:T(8,128)(2,1)S(1)}, bf16[128,256]{1,0:T(8,128)(2,1)}, u32[]{:S(2)}) %copy-start.3) | copy-done | bytes 65560
  4.0 0.0 copy-start.4
  4.0 0.7 %copy-done.4 = f32[3,512]{1,0:T(4,128)S(1)} copy-done((f32[3,512]{1,0:T(4,128)S(1)}, f32[3,512]{1,0:T(4,128)}, u32[]{:S(2)}) %copy-start.4) | copy-done | bytes 6168
  4.7 45.3 %shard_map.76 = (bf16[128,256]{1,0:T(8,128)(2,1)S(1)}, f32[3,128]{1,0:T(4,128)S(1)}, f32[128,256]{1,0:T(8,128)S(1)}) custom-call(f32[3,512]{1,0:T(4,128)S(1)} %copy-done.4, bf16[128,256]{1,0:T(8,128)(2,1)S(1)} %copy-done, bf16[128,256]{1,0:T(8,128)(2,1)S(1)} %copy-done.1, f32[3,4096]{1,0:T(4,128)S(1)} %copy-done.2, bf16[128,256]{1,0:T(8,128)(2,1)S(1)} %copy-done.3), custom_call_target="tpu_custom_call" | custom-call | tf_op jit(solution)/shard_map/pallas_call | solution.py:303
  50.0 0.6 %copy.11 = bf16[128,256]{1,0:T(8,128)(2,1)} copy(bf16[128,256]{1,0:T(8,128)(2,1)S(1)} %get-tuple-element.6) | data formatting | bytes 131072
  50.7 0.6 %copy.12 = f32[3,128]{1,0:T(4,128)} copy(f32[3,128]{1,0:T(4,128)S(1)} %get-tuple-element.7) | data formatting | bytes 3072
  51.3 0.7 %copy.13 = f32[128,256]{1,0:T(8,128)} copy(f32[128,256]{1,0:T(8,128)S(1)} %get-tuple-element.8) | data formatting | bytes 262144
Async XLA Ops:
  0.6 0.8 %copy-start = (bf16[128,256]{1,0:T(8,128)(2,1)S(1)}, bf16[128,256]{1,0:T(8,128)(2,1)}, u32[]{:S(2)}) copy-start(bf16[128,256]{1,0:T(8,128)(2,1)} %feat_ref.1) | copy-start | bytes 196612
  1.5 0.8 %copy-start.1 = (bf16[128,256]{1,0:T(8,128)(2,1)S(1)}, bf16[128,256]{1,0:T(8,128)(2,1)}, u32[]{:S(2)}) copy-start(bf16[128,256]{1,0:T(8,128)(2,1)} %cot_ref.1) | copy-start | bytes 196612
  2.3 0.8 %copy-start.2 = (f32[3,4096]{1,0:T(4,128)S(1)}, f32[3,4096]{1,0:T(4,128)}, u32[]{:S(2)}) copy-start(f32[3,4096]{1,0:T(4,128)} %kvec_ref.1) | copy-start | bytes 147460
  3.2 0.8 %copy-start.3 = (bf16[128,256]{1,0:T(8,128)(2,1)S(1)}, bf16[128,256]{1,0:T(8,128)(2,1)}, u32[]{:S(2)}) copy-start(bf16[128,256]{1,0:T(8,128)(2,1)} %gain_ref.1) | copy-start | bytes 196612
  4.0 0.7 %copy-start.4 = (f32[3,512]{1,0:T(4,128)S(1)}, f32[3,512]{1,0:T(4,128)}, u32[]{:S(2)}) copy-start(f32[3,512]{1,0:T(4,128)} %pos_ref.1) | copy-start | bytes 18436

commit v3 on v2

--- a/solution.py
+++ b/solution.py
@@ -330,7 +330,7 @@
             pltpu.VMEM((per, width), bf),
         ],
         compiler_params=pltpu.CompilerParams(
-            collective_id=0, has_side_effects=True, vmem_limit_bytes=40 << 20
+            collective_id=0, has_side_effects=True, vmem_limit_bytes=63 << 20
         ),
     )(positions, features, cotangent, wavevectors, filter_gain)
 

time: 52.3 us -> 49.6 us (0.948)
  local copies, waits for them, and re-layouts: 5.91 us -> 2.75 us
  Pallas kernels: 45.3 us -> 46.1 us
    unnamed x13 -> x7, local copies, waits for them, and re-layouts: 5.91 us -> 2.75 us
    pallas_call x1, Pallas kernels: 45.3 us -> 46.1 us  [fused(): pl.pallas_call(functools.partial(kernel, nz, spec_scale, wave_scale), out...]
where the time goes in v3:
time: 49.6 us; the launch traced here: 49.5 us
  Pallas kernels  46.1 us (93%)
  local copies, waits for them, and re-layouts  2.75 us (6%)
  between operations  0.66 us (1%)
    pallas_call x1, Pallas kernels, fused(): pl.pallas_call(functools.partial(kernel, nz, spec_scale, wave_scale), out...  46.1 us
    unnamed x7, local copies, waits for them, and re-layouts  2.75 us

profile of v3, /device:TPU:0, one launch (start us, length us, event | category | flops | bytes accessed | tf_op | source)
XLA Modules:
  0.0 49.5 jit_solution(5044819353362881669)
XLA Ops:
  0.6 46.1 %shard_map.76 = (bf16[128,256]{1,0:T(8,128)(2,1)}, f32[3,128]{1,0:T(4,128)}, f32[128,256]{1,0:T(8,128)}) custom-call(f32[3,512]{1,0:T(4,128)} %pos_ref.1, bf16[128,256]{1,0:T(8,128)(2,1)} %feat_ref.1, bf16[128,256]{1,0:T(8,128)(2,1)} %cot_ref.1, f32[3,4096]{1,0:T(4,128)} %kvec_ref.1, bf16[128,256]{1,0:T(8,128)(2,1)} %gain_ref.1), custom_call_target="tpu_custom_call" | custom-call | tf_op jit(solution)/shard_map/pallas_call | solution.py:303
  46.7 0.0 copy-start
  46.7 0.0 copy-start.1
  46.7 1.5 %copy.11 = bf16[128,256]{1,0:T(8,128)(2,1)} copy(bf16[128,256]{1,0:T(8,128)(2,1)} %get-tuple-element.6) | data formatting | bytes 131072
  48.2 0.0 copy-done.1
  48.2 0.6 %copy.12 = f32[3,128]{1,0:T(4,128)} copy(f32[3,128]{1,0:T(4,128)S(1)} %copy-done.1) | data formatting | bytes 3072
  48.8 0.0 copy-done
  48.8 0.7 %copy.13 = f32[128,256]{1,0:T(8,128)} copy(f32[128,256]{1,0:T(8,128)S(1)} %copy-done) | data formatting | bytes 262144
Async XLA Ops:
  46.7 2.1 %copy-start = (f32[128,256]{1,0:T(8,128)S(1)}, f32[128,256]{1,0:T(8,128)}, u32[]{:S(2)}) copy-start(f32[128,256]{1,0:T(8,128)} %get-tuple-element.8) | copy-start | bytes 393220
  46.7 1.5 %copy-start.1 = (f32[3,128]{1,0:T(4,128)S(1)}, f32[3,128]{1,0:T(4,128)}, u32[]{:S(2)}) copy-start(f32[3,128]{1,0:T(4,128)} %get-tuple-element.7) | copy-start | bytes 4612

commit v4 on v3

--- a/solution.py
+++ b/solution.py
@@ -200,10 +200,11 @@
     spread(2, False)
     for q in range(1, 5):
         arrive(3, q)
-    spread(3, False)
-
-    mid_tx[...] = acc[kk:, :].astype(jnp.bfloat16)
+    mid_tx[...] = (
+        acc[kk:, :] + jnp.dot(cs[3, kk:, :], joined[3], preferred_element_type=jnp.float32)
+    ).astype(jnp.bfloat16)
     first = send("m1", mid_tx, mid_rx, partner)
+    acc[:kk, :] += jnp.dot(cs[3, :kk, :], joined[3], preferred_element_type=jnp.float32)
     first.wait_recv()
     total = acc[:kk, :] + mid_rx[...].astype(jnp.float32)
     loads[4].wait()
@@ -216,8 +217,9 @@
     ebuf[per:kk, :width] = (gain * gi * spec_scale).astype(jnp.bfloat16)
     ebuf[per:kk, width:] = (gain * si * wave_scale).astype(jnp.bfloat16)
     second = send("m2", ebuf.at[:kk], ebuf.at[kk:], partner)
+    dt[:, :kk] = jnp.transpose(ebuf[:kk, :width].astype(jnp.float32)).astype(jnp.bfloat16)
     second.wait_recv()
-    dt[...] = jnp.transpose(ebuf[:, :width].astype(jnp.float32)).astype(jnp.bfloat16)
+    dt[:, kk:] = jnp.transpose(ebuf[kk:, :width].astype(jnp.float32)).astype(jnp.bfloat16)
 
     tall = pf.shape[2]
     cols = 2 * own

time: 49.6 us -> 49.7 us (level)
  no operation moved by 1% of the time
where the time goes in v4:
time: 49.7 us; the launch traced here: 49.5 us
  Pallas kernels  46.1 us (93%)
  local copies, waits for them, and re-layouts  2.75 us (6%)
  between operations  0.66 us (1%)
    pallas_call x1, Pallas kernels, fused(): pl.pallas_call(functools.partial(kernel, nz, spec_scale, wave_scale), out...  46.1 us
    unnamed x7, local copies, waits for them, and re-layouts  2.75 us

profile of v4, /device:TPU:0, one launch (start us, length us, event | category | flops | bytes accessed | tf_op | source)
XLA Modules:
  0.0 49.5 jit_solution(1786144782707985238)
XLA Ops:
  0.6 46.1 %shard_map.76 = (bf16[128,256]{1,0:T(8,128)(2,1)}, f32[3,128]{1,0:T(4,128)}, f32[128,256]{1,0:T(8,128)}) custom-call(f32[3,512]{1,0:T(4,128)} %pos_ref.1, bf16[128,256]{1,0:T(8,128)(2,1)} %feat_ref.1, bf16[128,256]{1,0:T(8,128)(2,1)} %cot_ref.1, f32[3,4096]{1,0:T(4,128)} %kvec_ref.1, bf16[128,256]{1,0:T(8,128)(2,1)} %gain_ref.1), custom_call_target="tpu_custom_call" | custom-call | tf_op jit(solution)/shard_map/pallas_call | solution.py:305
  46.8 0.0 copy-start
  46.8 0.0 copy-start.1
  46.8 1.5 %copy.11 = bf16[128,256]{1,0:T(8,128)(2,1)} copy(bf16[128,256]{1,0:T(8,128)(2,1)} %get-tuple-element.6) | data formatting | bytes 131072
  48.3 0.0 copy-done.1
  48.3 0.6 %copy.12 = f32[3,128]{1,0:T(4,128)} copy(f32[3,128]{1,0:T(4,128)S(1)} %copy-done.1) | data formatting | bytes 3072
  48.9 0.0 copy-done
  48.9 0.7 %copy.13 = f32[128,256]{1,0:T(8,128)} copy(f32[128,256]{1,0:T(8,128)S(1)} %copy-done) | data formatting | bytes 262144
Async XLA Ops:
  46.8 2.1 %copy-start = (f32[128,256]{1,0:T(8,128)S(1)}, f32[128,256]{1,0:T(8,128)}, u32[]{:S(2)}) copy-start(f32[128,256]{1,0:T(8,128)} %get-tuple-element.8) | copy-start | bytes 393220
  46.8 1.5 %copy-start.1 = (f32[3,128]{1,0:T(4,128)S(1)}, f32[3,128]{1,0:T(4,128)}, u32[]{:S(2)}) copy-start(f32[3,128]{1,0:T(4,128)} %get-tuple-element.7) | copy-start | bytes 4612
